TPU v7x, 32 devices: a whole 2x2x4 slice. The times are simulated.
32 devices in a mesh: tok: 4 (over y, core), exp: 8 (over z, x).
Axes of the slice: x: 2, y: 2, z: 4, core: 2. Of those that a mesh axis runs over, the one named last changes fastest.
Arguments:
- x_tokens: bfloat16 [4096, 4096], P(('tok', 'exp')), may hold values from -48 to 48
- router_weight: bfloat16 [4096, 512], replicated, may hold values from -1 to 1
- gate_rest: float32 [4096, 508], P(('tok', 'exp')), may hold values from -192 to 192
- latent_in: bfloat16 [4096, 1024], P(('tok', 'exp')), may hold values from -6 to 6
- latent_grad: bfloat16 [4096, 1024], P(('tok', 'exp')), may hold values from -6 to 6
- expert_picks: int32 [4096, 22], P('tok'), may hold values from 0 to 511, all different within a row; in each aligned block of 128 rows (0 to 127, 128 to 255, ...) at most 12 rows name the same one
- expert_in: bfloat16 [8, 1024, 1344], P('exp'), may hold values from -0.1875 to 0.1875
- expert_out: bfloat16 [8, 1344, 1024], P('exp'), may hold values from -0.125 to 0.125
Outputs:
- latent_in_grad: bfloat16 [4096, 1024], P(('tok', 'exp'))
- x_grad: bfloat16 [4096, 4096], P(('tok', 'exp'))
- router_weight_grad: float32 [4096, 512], P(('tok', 'exp'))
Inputs may be any that keep to these rules, and one draw needn't show every extreme that they name: `expert_picks`: each row names 22 different experts. Within each aligned block of 128 rows (the rows of one device) no expert is named more than 12 times, a bound that some block reaches; every expert is named somewhere.
All inputs are finite; a program needn't handle non-finite values.
Results may differ from a plain program's by a relative error of at most 0.009.
Values may be sent and summed in bfloat16 or wider, within the bound.
A program may use at most 128 MiB of HBM per device.

v0:
```python
import functools
import jax
import jax.numpy as jnp
from jax import lax
from jax.experimental import pallas as pl
from jax.experimental.pallas import tpu as pltpu
from jax.sharding import PartitionSpec as P

MESH = pl.DeviceIdType.MESH
F32 = jnp.float32
BF16 = jnp.bfloat16
NT = (((1,), (1,)), ((), ()))
SLOTS = 16


def kernel(
    toks, lanes, window,
    x_ref, gate_ref, latin_ref, latgrad_ref, picks_ref, rw_hbm, win_hbm, wout_hbm,
    latent_out, xgrad_out, rwg_out,
    rw, win, wout, lat, probs, pick_recv, pick_send, gate_recv, gate_send, gate_rows, gate_grads, hits_ref, own_hits_ref, rank, packed, active_ref,
    term_send, term_recv, xband, xturned, logits_all, part, ax_send, ax_recv,
    bz_send, bz_recv, bx_send, bx_recv, az_send, az_recv, total_a, total_b,
    load_sem, send_lat, chain_ss, recv_z, recv_x, pick_ss, pick_rs, gate_ss, gate_rs, term_ss, term_rs,
    band_ss, band_rs, log_ss, log_rs, ax_ss, ax_rs, bz_ss, bz_rs, bx_ss, bx_rs,
    az_ss, az_rs,
):
    tok = lax.axis_index("tok")
    lane = lax.axis_index("exp")
    outers = lanes // 2
    outer = lane // 2
    inner = lane % 2
    expert = lane // 2
    rows = x_ref.shape[0]
    feats = x_ref.shape[1] // toks
    half = feats // lanes // 2

    loads = [
        pltpu.make_async_copy(rw_hbm, rw, load_sem.at[0]),
        pltpu.make_async_copy(win_hbm.at[0], win, load_sem.at[1]),
        pltpu.make_async_copy(wout_hbm.at[0], wout, load_sem.at[2]),
    ]
    for load in loads:
        load.start()

    def at_lane(k):
        return lax.rem(lane + k, lanes)

    def at_tok(k):
        return lax.rem(tok + k, toks)

    barrier = pltpu.get_barrier_semaphore()
    for k in range(1, lanes):
        pl.semaphore_signal(barrier, inc=1, device_id={"exp": at_lane(k)}, device_id_type=MESH)
    for k in range(1, toks):
        pl.semaphore_signal(barrier, inc=1, device_id={"tok": at_tok(k)}, device_id_type=MESH)
    lat[0, lane] = latin_ref[...]
    lat[1, lane] = latgrad_ref[...]
    pl.semaphore_wait(barrier, lanes - 1 + toks - 1)

    def lat_copy(kind, which, src_outer, src_inner):
        slot = src_outer * 2 + src_inner
        if kind == 2:
            peer, recv = outer * 2 + 1 - inner, recv_x.at[which, src_outer]
        else:
            peer, recv = lane + (2 if kind == 0 else -2), recv_z.at[which, src_outer]
        return pltpu.make_async_remote_copy(
            src_ref=lat.at[which, slot], dst_ref=lat.at[which, slot],
            send_sem=send_lat.at[kind, which, src_outer], recv_sem=recv,
            device_id={"exp": peer}, device_id_type=MESH,
        )

    def forward(which, src_outer, do):
        @pl.when((src_outer <= outer) & (outer < outers - 1))
        def _():
            do(lat_copy(0, which, src_outer, inner))

        @pl.when((src_outer >= outer) & (outer > 0))
        def _():
            do(lat_copy(1, which, src_outer, inner))

        if which == 0:
            do(lat_copy(2, which, src_outer, inner))
        else:
            @pl.when((src_outer == outer) | ((src_outer > 0) & (src_outer < outers - 1)))
            def _():
                do(lat_copy(2, which, src_outer, inner))

    def chain(src_outer, do):
        slot = src_outer * 2 + 1 - inner
        for side, end in ((1, 0), (-1, outers - 1)):
            @pl.when((src_outer == end) & (outer + side >= 0) & (outer + side < outers))
            def _():
                do(pltpu.make_async_remote_copy(
                    src_ref=lat.at[1, slot], dst_ref=lat.at[1, slot],
                    send_sem=chain_ss.at[0 if side == 1 else 1], recv_sem=recv_x.at[1, src_outer],
                    device_id={"exp": lane + 2 * side}, device_id_type=MESH,
                ))

    for which in range(2):
        forward(which, outer, lambda c: c.start())

    def band_copy(k):
        peer = at_tok(k)
        return pltpu.make_async_remote_copy(
            src_ref=x_ref.at[:, pl.ds(pl.multiple_of(peer * feats, 128), feats)],
            dst_ref=xband.at[tok],
            send_sem=band_ss.at[k], recv_sem=band_rs.at[toks - k],
            device_id={"tok": peer}, device_id_type=MESH,
        )

    for k in range(1, toks):
        band_copy(k).start()
    xband[tok] = x_ref[:, pl.ds(pl.multiple_of(tok * feats, 128), feats)]

    def any_row(picks, e):
        return jnp.max((picks == e).astype(F32), axis=0, keepdims=True)

    group_hits = any_row(picks_ref[...], expert)
    for k in range(lanes):
        hits_ref[k:k + 1, :] = group_hits[:, k * rows:(k + 1) * rows]
    own_picks = picks_ref[:, pl.ds(pl.multiple_of(lane * rows, rows), rows)]
    own_hits_ref[...] = jnp.zeros_like(own_hits_ref)
    for e in range(window):
        own_hits_ref[e:e + 1, :] = any_row(own_picks, e)
    rest = gate_ref.shape[1]
    gate_grads[:, rest - rest % 128:] = jnp.zeros_like(gate_grads[:, rest - rest % 128:])
    gate_grads[:, :rest] = gate_ref[...]
    gate_grads[...] = pltpu.roll(gate_grads[...], window, 1)

    loads[0].wait()
    logits = jnp.dot(x_ref[...], rw[...], preferred_element_type=F32)
    shifted = jnp.exp(logits - jnp.max(logits, axis=1, keepdims=True))
    probs[...] = shifted / jnp.sum(shifted, axis=1, keepdims=True)
    pad = own_hits_ref.shape[0]
    pick_send[...] = jnp.transpose(probs[:, :128])[:pad] * own_hits_ref[...]
    pick_recv[0] = pick_send[...]

    def pick_copy(k):
        return pltpu.make_async_remote_copy(
            src_ref=pick_send, dst_ref=pick_recv.at[lanes - k],
            send_sem=pick_ss.at[k], recv_sem=pick_rs.at[lanes - k],
            device_id={"exp": at_lane(k)}, device_id_type=MESH,
        )

    for k in range(1, lanes):
        pick_copy(k).start()
    before = (
        lax.broadcasted_iota(jnp.int32, (rows, rows), 0)
        <= lax.broadcasted_iota(jnp.int32, (rows, rows), 1)
    ).astype(BF16)
    rank[...] = jnp.dot(hits_ref[...].astype(BF16), before, preferred_element_type=F32) - 1.0
    slot_iota = lax.broadcasted_iota(jnp.int32, (SLOTS, rows), 0).astype(F32)
    loads[1].wait()
    loads[2].wait()
    for k in range(1, lanes):
        pick_copy(k).wait_recv()

    def gate_copy(src_lane):
        return pltpu.make_async_remote_copy(
            src_ref=gate_send.at[src_lane], dst_ref=gate_recv.at[lane],
            send_sem=gate_ss.at[src_lane], recv_sem=gate_rs.at[lane],
            device_id={"exp": src_lane}, device_id_type=MESH,
        )

    def pair_rows(src_outer, wait_for):
        first = src_outer * 2
        both = lat.shape[3]
        wait_for(0)
        rows_in = lat[0, pl.ds(first, 2)].reshape(2 * rows, both)
        active_ref[...] = jnp.maximum(lax.dot_general(rows_in, win[...], NT, preferred_element_type=F32), 0.0)
        wait_for(1)
        rows_grad = lat[1, pl.ds(first, 2)].reshape(2 * rows, both)
        grad = lax.dot_general(rows_grad, wout[...], NT, preferred_element_type=F32)
        active = active_ref[...]
        product = active * grad
        gate = jnp.sum(active * product, axis=1, keepdims=True)
        gate_row = jnp.transpose(jnp.broadcast_to(gate, (2 * rows, 128)))[:8]
        for side in range(2):
            gate_send[first + side] = gate_row[:, side * rows:(side + 1) * rows]

            @pl.when(first + side == lane)
            def _():
                gate_recv[lane] = gate_row[:, side * rows:(side + 1) * rows]

            @pl.when(first + side != lane)
            def _():
                gate_copy(first + side).start()

        raw_rows = (2.0 * product).astype(BF16)
        for side in range(2):
            src_lane = first + side
            chosen = (
                (hits_ref[pl.ds(src_lane, 1), :] > 0.0) & (rank[pl.ds(src_lane, 1), :] == slot_iota)
            ).astype(F32)
            picked = pick_recv[lax.rem(src_lane - lane + lanes, lanes), pl.ds(expert, 1), :]
            scale = jnp.sum(chosen * picked, axis=1, keepdims=True)
            raw = jnp.dot(
                chosen.astype(BF16), raw_rows[side * rows:(side + 1) * rows], preferred_element_type=F32
            )
            packed[src_lane] = (raw * scale).astype(BF16)

    def arrivals(step, carry):
        for side in (-1, 1):
            src_outer = outer + side * step

            @pl.when((step > 0) & (step < outers) & (src_outer >= 0) & (src_outer < outers))
            def _():
                for which in range(2):
                    lat_copy(0, which, src_outer, inner).wait_recv()
                    forward(which, src_outer, lambda c: c.start())

        def pair(q, carry):
            distance = step - 1
            src_outer = outer + (2 * q - 1) * distance
            valid = (src_outer >= 0) & (src_outer < outers) & (distance >= 0)
            valid = valid & ((distance > 0) | (q == 0))

            @pl.when(valid)
            def _():
                def wait_for(which):
                    lat_copy(2, which, src_outer, 1 - inner).wait_recv()
                    if which == 1:
                        chain(src_outer, lambda c: c.start())

                pair_rows(src_outer, wait_for)

            return carry

        lax.fori_loop(0, 2, pair, 0)

        @pl.when(step == outers - 1)
        def _():
            for k in range(toks):
                if k:
                    band_copy(k).wait_recv()
            for k in range(toks):
                xturned[:, k * rows:(k + 1) * rows] = jnp.transpose(xband[k])

        return carry

    lax.fori_loop(0, outers + 1, arrivals, 0)

    for k in range(1, lanes):
        peer = at_lane(k)
        pltpu.make_async_remote_copy(
            src_ref=gate_send.at[peer], dst_ref=gate_recv.at[peer],
            send_sem=gate_ss.at[peer], recv_sem=gate_rs.at[peer],
            device_id={"exp": peer}, device_id_type=MESH,
        ).wait_recv()
    gate_rows[...] = jnp.zeros_like(gate_rows)
    for e in range(window):
        gate_rows[e:e + 1, :] = gate_recv[2 * e, 0:1, :] + gate_recv[2 * e + 1, 0:1, :]
    gate_grads[:, :128] = gate_grads[:, :128] + jnp.transpose(gate_rows[...])
    gate_grad = gate_grads[...]
    prob = probs[...]
    centre = jnp.sum(prob * gate_grad, axis=1, keepdims=True)
    logit_low = (prob * (gate_grad - centre)).astype(BF16)
    logits_all[tok] = logit_low
    sibling = tok + 1 - 2 * lax.rem(tok, 2)

    def logit_copy(to_sibling, k):
        far = lax.rem(tok + 2 * k, toks)
        src = far if to_sibling else tok
        sem = (toks // 2 + k) if to_sibling else (toks // 2 - k) % (toks // 2)
        return pltpu.make_async_remote_copy(
            src_ref=logits_all.at[src], dst_ref=logits_all.at[src],
            send_sem=log_ss.at[toks // 2 + k if to_sibling else k], recv_sem=log_rs.at[sem],
            device_id={"tok": sibling if to_sibling else far}, device_id_type=MESH,
        )

    for k in range(1, toks // 2):
        logit_copy(False, k).start()
    logit_copy(True, 0).start()

    terms = jnp.dot(
        packed[...].reshape(lanes * SLOTS, packed.shape[2]), win[...], preferred_element_type=F32
    )
    term_send[...] = terms.astype(BF16).reshape(term_send.shape)

    def term_copy(k):
        return pltpu.make_async_remote_copy(
            src_ref=term_send.at[at_lane(k)], dst_ref=term_recv.at[lane],
            send_sem=term_ss.at[k], recv_sem=term_rs.at[lanes - k],
            device_id={"exp": at_lane(k)}, device_id_type=MESH,
        )

    for k in range(1, lanes):
        term_copy(k).start()
    term_recv[lane] = term_send[lane]

    for k in range(toks // 2 - 1, 0, -1):
        logit_copy(False, toks // 2 - k).wait_recv()
        logit_copy(True, k).start()
    for k in range(toks // 2):
        logit_copy(True, k).wait_recv()

    experts = rw.shape[1]
    part[...] = jnp.dot(
        xturned[...], logits_all[...].reshape(toks * rows, experts), preferred_element_type=F32
    ).reshape(part.shape)
    neighbour = outer * 2 + 1 - inner

    def ax_copy(d):
        return pltpu.make_async_remote_copy(
            src_ref=ax_send.at[d], dst_ref=ax_recv.at[d], send_sem=ax_ss.at[d], recv_sem=ax_rs.at[d],
            device_id={"exp": neighbour}, device_id_type=MESH,
        )

    for d in range(outers):
        ax_send[d] = part[d, 1 - inner, :half].astype(BF16)
        ax_copy(d).start()

    def line_copy(send, recv, ss, rs, way, side, d):
        return pltpu.make_async_remote_copy(
            src_ref=send.at[way, d], dst_ref=recv.at[way, d], send_sem=ss.at[way, d],
            recv_sem=rs.at[way, d], device_id={"exp": lane + 2 * side}, device_id_type=MESH,
        )

    def line_item(m):
        j, q = m // 2, m % 2
        side = (1 - 2 * ((outer * 2) // outers)) * (1 - 2 * q)
        d = ((side + 1) // 2) * (outers - 1 - 2 * j) + j
        return (1 - side) // 2, side, d

    def line(send, recv, ss, rs, own):
        def item(m, carry):
            way, side, d = line_item(m)
            ahead = (d - outer) * side > 0
            behind = (outer - side >= 0) & (outer - side < outers)

            @pl.when(ahead & behind)
            def _():
                line_copy(send, recv, ss, rs, way, side, d).wait_recv()
                send[way, d] = (own(d) + recv[way, d].astype(F32)).astype(BF16)

            @pl.when(ahead & jnp.logical_not(behind))
            def _():
                send[way, d] = own(d).astype(BF16)

            @pl.when(ahead)
            def _():
                line_copy(send, recv, ss, rs, way, side, d).start()

            return carry

        lax.fori_loop(0, 2 * outers, item, 0)

    def line_end(send, recv, ss, rs, total):
        for way, side in ((0, 1), (1, -1)):
            @pl.when((outer - side >= 0) & (outer - side < outers))
            def _():
                line_copy(send, recv, ss, rs, way, side, outer).wait_recv()
                total[...] = total[...] + recv[way, outer].astype(F32)

    def line_sent(send, recv, ss, rs):
        def item(m, carry):
            way, side, d = line_item(m)

            @pl.when((d - outer) * side > 0)
            def _():
                line_copy(send, recv, ss, rs, way, side, d).wait_send()

            return carry

        lax.fori_loop(0, 2 * outers, item, 0)

    line_b = (bz_send, bz_recv, bz_ss, bz_rs)
    line_a = (az_send, az_recv, az_ss, az_rs)
    line(*line_b, lambda d: part[d, :, half:])
    for d in range(outers):
        ax_copy(d).wait_recv()
        part[d, inner, :half] = part[d, inner, :half] + ax_recv[d].astype(F32)
    line(*line_a, lambda d: part[d, inner, :half])
    total_b[...] = part[outer, :, half:]
    line_end(*line_b, total_b)
    bx_send[...] = total_b[1 - inner].astype(BF16)
    bx = pltpu.make_async_remote_copy(
        src_ref=bx_send, dst_ref=bx_recv, send_sem=bx_ss, recv_sem=bx_rs,
        device_id={"exp": neighbour}, device_id_type=MESH,
    )
    bx.start()

    for k in range(1, lanes):
        peer = at_lane(k)
        pltpu.make_async_remote_copy(
            src_ref=term_send.at[peer], dst_ref=term_recv.at[peer],
            send_sem=term_ss.at[k], recv_sem=term_rs.at[k],
            device_id={"exp": peer}, device_id_type=MESH,
        ).wait_recv()
    own_hits = own_hits_ref[...]
    own_rank = jnp.dot(own_hits.astype(BF16), before, preferred_element_type=F32) - 1.0
    spread = []
    for e in range(window):
        block = ((own_hits[e:e + 1] > 0.0) & (own_rank[e:e + 1] == slot_iota)).astype(F32)
        spread += [block, block]
    spread = jnp.transpose(jnp.concatenate(spread, axis=0)).astype(BF16)
    latent_out[...] = jnp.dot(
        spread, term_recv[...].reshape(lanes * SLOTS, term_recv.shape[2]), preferred_element_type=F32
    ).astype(BF16)

    xgrad_out[...] = lax.dot_general(logit_low, rw[...], NT, preferred_element_type=F32).astype(BF16)

    total_a[...] = part[outer, inner, :half]
    line_end(*line_a, total_a)
    rwg_out[:half] = total_a[...]
    bx.wait_recv()
    rwg_out[half:] = total_b[inner] + bx_recv[...].astype(F32)

    def sent(src_outer, carry):
        for which in range(2):
            forward(which, src_outer, lambda c: c.wait_send())
        chain(src_outer, lambda c: c.wait_send())
        return carry

    lax.fori_loop(0, outers, sent, 0)
    for k in range(1, lanes):
        pick_copy(k).wait_send()
        gate_copy(at_lane(k)).wait_send()
        term_copy(k).wait_send()
    for k in range(1, toks):
        band_copy(k).wait_send()
    for d in range(outers):
        ax_copy(d).wait_send()
    line_sent(*line_b)
    line_sent(*line_a)
    bx.wait_send()
    for k in range(toks // 2):
        logit_copy(True, k).wait_send()
        if k:
            logit_copy(False, k).wait_send()


def hand_over(*refs):
    count = len(refs) // 3
    sems = refs[-1]
    ins, outs, held = refs[:count], refs[count:2 * count], refs[2 * count:3 * count]
    loads = [pltpu.make_async_copy(ins[k], held[k], sems.at[k]) for k in range(count)]
    stores = [pltpu.make_async_copy(held[k], outs[k], sems.at[count + k]) for k in range(count)]
    for load in loads:
        load.start()
    for load, store in zip(loads, stores):
        load.wait()
        store.start()
    for store in stores:
        store.wait()


def shards(
    x_tokens, router_weight, gate_rest, latent_in, latent_grad, expert_picks, expert_in, expert_out
):
    toks = lax.axis_size("tok")
    lanes = lax.axis_size("exp")
    rows, width = x_tokens.shape
    experts = router_weight.shape[1]
    window = experts - gate_rest.shape[1]
    latent, hidden = expert_in.shape[1:]
    feats = width // toks
    own_rows = feats // lanes
    outers = lanes // 2
    half = own_rows // 2
    pad = -(-window // 8) * 8
    vmem = pl.BlockSpec(memory_space=pltpu.VMEM)
    anywhere = pl.BlockSpec(memory_space=pl.ANY)
    dma = pltpu.SemaphoreType.DMA
    results = pl.pallas_call(
        functools.partial(kernel, toks, lanes, window),
        out_shape=(
            jax.ShapeDtypeStruct((rows, latent), BF16),
            jax.ShapeDtypeStruct((rows, width), BF16),
            jax.ShapeDtypeStruct((own_rows, experts), F32),
        ),
        in_specs=[vmem] * 5 + [anywhere] * 3,
        out_specs=(vmem, vmem, vmem),
        scratch_shapes=[
            pltpu.VMEM((width, experts), BF16),
            pltpu.VMEM((hidden, latent), BF16),
            pltpu.VMEM((hidden, latent), BF16),
            pltpu.VMEM((2, lanes, rows, latent), BF16),
            pltpu.VMEM((rows, experts), F32),
            pltpu.VMEM((lanes, pad, rows), F32),
            pltpu.VMEM((pad, rows), F32),
            pltpu.VMEM((lanes, 8, rows), F32),
            pltpu.VMEM((lanes, 8, rows), F32),
            pltpu.VMEM((128, rows), F32),
            pltpu.VMEM((rows, experts), F32),
            pltpu.VMEM((lanes, rows), F32),
            pltpu.VMEM((pad, rows), F32),
            pltpu.VMEM((lanes, rows), F32),
            pltpu.VMEM((lanes, SLOTS, hidden), BF16),
            pltpu.VMEM((2 * rows, hidden), F32),
            pltpu.VMEM((lanes, SLOTS, latent), BF16),
            pltpu.VMEM((lanes, SLOTS, latent), BF16),
            pltpu.VMEM((toks, rows, feats), BF16),
            pltpu.VMEM((feats, toks * rows), BF16),
            pltpu.VMEM((toks, rows, experts), BF16),
            pltpu.VMEM((outers, 2, own_rows, experts), F32),
            pltpu.VMEM((outers, half, experts), BF16),
            pltpu.VMEM((outers, half, experts), BF16),
            pltpu.VMEM((2, outers, 2, half, experts), BF16),
            pltpu.VMEM((2, outers, 2, half, experts), BF16),
            pltpu.VMEM((half, experts), BF16),
            pltpu.VMEM((half, experts), BF16),
            pltpu.VMEM((2, outers, half, experts), BF16),
            pltpu.VMEM((2, outers, half, experts), BF16),
            pltpu.VMEM((half, experts), F32),
            pltpu.VMEM((2, half, experts), F32),
            dma((3,)),
            dma((3, 2, outers)),
            dma((2,)),
            dma((2, outers)),
            dma((2, outers)),
            dma((lanes,)), dma((lanes,)),
            dma((lanes,)), dma((lanes,)),
            dma((lanes,)), dma((lanes,)),
            dma((toks,)), dma((toks,)),
            dma((toks,)), dma((toks,)),
            dma((outers,)), dma((outers,)),
            dma((2, outers)), dma((2, outers)),
            dma, dma,
            dma((2, outers)), dma((2, outers)),
        ],
        compiler_params=pltpu.CompilerParams(
            collective_id=0, has_side_effects=True, vmem_limit_bytes=56 * 1024 * 1024
        ),
    )(
        x_tokens, gate_rest, latent_in, latent_grad, expert_picks.T, router_weight,
        jnp.swapaxes(expert_in, 1, 2), expert_out,
    )
    return pl.pallas_call(
        hand_over,
        out_shape=tuple(jax.ShapeDtypeStruct(r.shape, r.dtype) for r in results),
        in_specs=[anywhere] * len(results),
        out_specs=(anywhere,) * len(results),
        scratch_shapes=[pltpu.VMEM(r.shape, r.dtype) for r in results] + [dma((2 * len(results),))],
    )(*results)


def solution(mesh):
    placed = (
        P(("tok", "exp"), None),
        P(),
        P(("tok", "exp"), None),
        P(("tok", "exp"), None),
        P(("tok", "exp"), None),
        P("tok", None),
        P("exp", None, None),
        P("exp", None, None),
    )
    return jax.shard_map(
        shards,
        mesh=mesh,
        in_specs=placed,
        out_specs=(P(("tok", "exp"), None), P(("tok", "exp"), None), P(("tok", "exp"), None)),
        check_vma=False,
    )
```

profile of v0, /device:TPU:0, one launch (start us, length us, event | category | flops | bytes accessed | tf_op | source)
XLA Modules:
  0.0 89.4 jit_solution(2809850064064296466)
XLA Ops:
  0.6 86.3 %shard_map.103 = (bf16[128,1024]{1,0:T(8,128)(2,1)}, bf16[128,4096]{1,0:T(8,128)(2,1)}, f32[128,512]{1,0:T(8,128)}) custom-call(bf16[128,4096]{1,0:T(8,128)(2,1)} %x_ref.1, f32[128,508]{1,0:T(8,128)} %gate_ref.1, bf16[128,1024]{1,0:T(8,128)(2,1)} %latin_ref.1, bf16[128,1024]{1,0:T(8,128)(2,1)} %latgrad_ref.1, s32[22,1024]{1,0:T(8,128)} %bitcast.3, ...), custom_call_target="tpu_custom_call" | custom-call | tf_op jit(solution)/shard_map/pallas_call | solution.py:465
  87.0 2.4 %shard_map.104 = (bf16[128,1024]{1,0:T(8,128)(2,1)}, bf16[128,4096]{1,0:T(8,128)(2,1)}, f32[128,512]{1,0:T(8,128)}) custom-call(bf16[128,1024]{1,0:T(8,128)(2,1)} %get-tuple-element.6.refs_0_, bf16[128,4096]{1,0:T(8,128)(2,1)} %get-tuple-element.7.refs_1_, f32[128,512]{1,0:T(8,128)} %get-tuple-element.8.refs_2_), custom_call_target="tpu_custom_call" | custom-call | tf_op jit(solution)/shard_map/pallas_call | solution.py:529
where the time goes:
time: 89.5 us; the launch traced here: 89.4 us
  Pallas kernels  88.7 us (99%)
    pallas_call x1, Pallas kernels, shards(): pl.pallas_call(functools.partial(kernel, toks, lanes, window), out_shape=...  86.3 us
    pallas_call x1, Pallas kernels, shards(): pl.pallas_call(hand_over, out_shape=tuple((jax.ShapeDtypeStruct(r.shape,...  2.41 us

commit v1 on v0

--- a/solution.py
+++ b/solution.py
@@ -15,8 +15,9 @@
 
 def kernel(
     toks, lanes, window,
-    x_ref, gate_ref, latin_ref, latgrad_ref, picks_ref, rw_hbm, win_hbm, wout_hbm,
-    latent_out, xgrad_out, rwg_out,
+    x_hbm, gate_hbm, latin_hbm, latgrad_hbm, picks_hbm, rw_hbm, win_hbm, wout_hbm,
+    latent_hbm, xgrad_hbm, rwg_out,
+    x_ref, gate_ref, picks_ref, latent_out, xgrad_out,
     rw, win, wout, lat, probs, pick_recv, pick_send, gate_recv, gate_send, gate_rows, gate_grads, hits_ref, own_hits_ref, rank, packed, active_ref,
     term_send, term_recv, xband, xturned, logits_all, part, ax_send, ax_recv,
     bz_send, bz_recv, bx_send, bx_recv, az_send, az_recv, total_a, total_b,
@@ -31,15 +32,27 @@
     inner = lane % 2
     expert = lane // 2
     rows = x_ref.shape[0]
+    own_rows = rwg_out.shape[0]
     feats = x_ref.shape[1] // toks
-    half = feats // lanes // 2
-
+    half = ax_send.shape[1]
+
+    first_loads = [
+        pltpu.make_async_copy(latin_hbm, lat.at[0, lane], load_sem.at[3]),
+        pltpu.make_async_copy(latgrad_hbm, lat.at[1, lane], load_sem.at[4]),
+        pltpu.make_async_copy(x_hbm, x_ref, load_sem.at[5]),
+        pltpu.make_async_copy(picks_hbm, picks_ref, load_sem.at[6]),
+        pltpu.make_async_copy(gate_hbm, gate_ref, load_sem.at[7]),
+    ]
     loads = [
         pltpu.make_async_copy(rw_hbm, rw, load_sem.at[0]),
         pltpu.make_async_copy(win_hbm.at[0], win, load_sem.at[1]),
         pltpu.make_async_copy(wout_hbm.at[0], wout, load_sem.at[2]),
     ]
-    for load in loads:
+    stores = [
+        pltpu.make_async_copy(latent_out, latent_hbm, load_sem.at[8]),
+        pltpu.make_async_copy(xgrad_out, xgrad_hbm, load_sem.at[9]),
+    ]
+    for load in first_loads + loads:
         load.start()
 
     def at_lane(k):
@@ -53,8 +66,8 @@
         pl.semaphore_signal(barrier, inc=1, device_id={"exp": at_lane(k)}, device_id_type=MESH)
     for k in range(1, toks):
         pl.semaphore_signal(barrier, inc=1, device_id={"tok": at_tok(k)}, device_id_type=MESH)
-    lat[0, lane] = latin_ref[...]
-    lat[1, lane] = latgrad_ref[...]
+    first_loads[0].wait()
+    first_loads[1].wait()
     pl.semaphore_wait(barrier, lanes - 1 + toks - 1)
 
     def lat_copy(kind, which, src_outer, src_inner):
@@ -108,6 +121,8 @@
             device_id={"tok": peer}, device_id_type=MESH,
         )
 
+    for load in first_loads[2:]:
+        load.wait()
     for k in range(1, toks):
         band_copy(k).start()
     xband[tok] = x_ref[:, pl.ds(pl.multiple_of(tok * feats, 128), feats)]
@@ -209,6 +224,14 @@
                     lat_copy(0, which, src_outer, inner).wait_recv()
                     forward(which, src_outer, lambda c: c.start())
 
+        for side in (-1, 1):
+            far = outer + side * (step - 1)
+
+            @pl.when((step > 0) & ((step > 1) | (side == 1)) & ((far == 0) | (far == outers - 1)))
+            def _():
+                lat_copy(2, 1, far, 1 - inner).wait_recv()
+                chain(far, lambda c: c.start())
+
         def pair(q, carry):
             distance = step - 1
             src_outer = outer + (2 * q - 1) * distance
@@ -218,9 +241,12 @@
             @pl.when(valid)
             def _():
                 def wait_for(which):
-                    lat_copy(2, which, src_outer, 1 - inner).wait_recv()
-                    if which == 1:
-                        chain(src_outer, lambda c: c.start())
+                    if which == 0:
+                        lat_copy(2, which, src_outer, 1 - inner).wait_recv()
+                    else:
+                        @pl.when((src_outer > 0) & (src_outer < outers - 1))
+                        def _():
+                            lat_copy(2, which, src_outer, 1 - inner).wait_recv()
 
                 pair_rows(src_outer, wait_for)
 
@@ -306,10 +332,6 @@
             device_id={"exp": neighbour}, device_id_type=MESH,
         )
 
-    for d in range(outers):
-        ax_send[d] = part[d, 1 - inner, :half].astype(BF16)
-        ax_copy(d).start()
-
     def line_copy(send, recv, ss, rs, way, side, d):
         return pltpu.make_async_remote_copy(
             src_ref=send.at[way, d], dst_ref=recv.at[way, d], send_sem=ss.at[way, d],
@@ -322,12 +344,34 @@
         d = ((side + 1) // 2) * (outers - 1 - 2 * j) + j
         return (1 - side) // 2, side, d
 
-    def line(send, recv, ss, rs, own):
+    def ax_start(m, carry):
+        way, side, d = line_item(m)
+
+        @pl.when((d - outer) * side > 0)
+        def _():
+            ax_send[d] = part[d, 1 - inner, :half].astype(BF16)
+            ax_copy(d).start()
+
+        return carry
+
+    lax.fori_loop(0, 2 * outers, ax_start, 0)
+    ax_send[outer] = part[outer, 1 - inner, :half].astype(BF16)
+    ax_copy(outer).start()
+
+    def ax_wait(d):
+        ax_copy(d).wait_recv()
+        part[d, inner, :half] = part[d, inner, :half] + ax_recv[d].astype(F32)
+
+    def line(send, recv, ss, rs, own, ready):
         def item(m, carry):
             way, side, d = line_item(m)
             ahead = (d - outer) * side > 0
             behind = (outer - side >= 0) & (outer - side < outers)
 
+            @pl.when(ahead)
+            def _():
+                ready(d)
+
             @pl.when(ahead & behind)
             def _():
                 line_copy(send, recv, ss, rs, way, side, d).wait_recv()
@@ -366,11 +410,8 @@
 
     line_b = (bz_send, bz_recv, bz_ss, bz_rs)
     line_a = (az_send, az_recv, az_ss, az_rs)
-    line(*line_b, lambda d: part[d, :, half:])
-    for d in range(outers):
-        ax_copy(d).wait_recv()
-        part[d, inner, :half] = part[d, inner, :half] + ax_recv[d].astype(F32)
-    line(*line_a, lambda d: part[d, inner, :half])
+    line(*line_b, lambda d: part[d, :, half:], lambda d: None)
+    line(*line_a, lambda d: part[d, inner, :half], ax_wait)
     total_b[...] = part[outer, :, half:]
     line_end(*line_b, total_b)
     bx_send[...] = total_b[1 - inner].astype(BF16)
@@ -398,14 +439,19 @@
         spread, term_recv[...].reshape(lanes * SLOTS, term_recv.shape[2]), preferred_element_type=F32
     ).astype(BF16)
 
+    stores[0].start()
     xgrad_out[...] = lax.dot_general(logit_low, rw[...], NT, preferred_element_type=F32).astype(BF16)
-
+    stores[1].start()
+
+    ax_wait(outer)
     total_a[...] = part[outer, inner, :half]
     line_end(*line_a, total_a)
     rwg_out[:half] = total_a[...]
     bx.wait_recv()
     rwg_out[half:] = total_b[inner] + bx_recv[...].astype(F32)
 
+    for store in stores:
+        store.wait()
     def sent(src_outer, carry):
         for which in range(2):
             forward(which, src_outer, lambda c: c.wait_send())
@@ -457,7 +503,8 @@
     feats = width // toks
     own_rows = feats // lanes
     outers = lanes // 2
-    half = own_rows // 2
+    half = max(16, own_rows * 3 // 4 // 16 * 16)
+    tail = own_rows - half
     pad = -(-window // 8) * 8
     vmem = pl.BlockSpec(memory_space=pltpu.VMEM)
     anywhere = pl.BlockSpec(memory_space=pl.ANY)
@@ -469,9 +516,14 @@
             jax.ShapeDtypeStruct((rows, width), BF16),
             jax.ShapeDtypeStruct((own_rows, experts), F32),
         ),
-        in_specs=[vmem] * 5 + [anywhere] * 3,
-        out_specs=(vmem, vmem, vmem),
+        in_specs=[anywhere] * 8,
+        out_specs=(anywhere, anywhere, vmem),
         scratch_shapes=[
+            pltpu.VMEM((rows, width), BF16),
+            pltpu.VMEM(gate_rest.shape, F32),
+            pltpu.VMEM((expert_picks.shape[1], expert_picks.shape[0]), jnp.int32),
+            pltpu.VMEM((rows, latent), BF16),
+            pltpu.VMEM((rows, width), BF16),
             pltpu.VMEM((width, experts), BF16),
             pltpu.VMEM((hidden, latent), BF16),
             pltpu.VMEM((hidden, latent), BF16),
@@ -496,15 +548,15 @@
             pltpu.VMEM((outers, 2, own_rows, experts), F32),
             pltpu.VMEM((outers, half, experts), BF16),
             pltpu.VMEM((outers, half, experts), BF16),
-            pltpu.VMEM((2, outers, 2, half, experts), BF16),
-            pltpu.VMEM((2, outers, 2, half, experts), BF16),
-            pltpu.VMEM((half, experts), BF16),
-            pltpu.VMEM((half, experts), BF16),
+            pltpu.VMEM((2, outers, 2, tail, experts), BF16),
+            pltpu.VMEM((2, outers, 2, tail, experts), BF16),
+            pltpu.VMEM((tail, experts), BF16),
+            pltpu.VMEM((tail, experts), BF16),
             pltpu.VMEM((2, outers, half, experts), BF16),
             pltpu.VMEM((2, outers, half, experts), BF16),
             pltpu.VMEM((half, experts), F32),
-            pltpu.VMEM((2, half, experts), F32),
-            dma((3,)),
+            pltpu.VMEM((2, tail, experts), F32),
+            dma((10,)),
             dma((3, 2, outers)),
             dma((2,)),
             dma((2, outers)),

time: 89.5 us -> 85.1 us (0.951)
  Pallas kernels: 88.7 us -> 84.4 us
    pallas_call x1, Pallas kernels: 86.3 us -> 81.9 us  [shards(): pl.pallas_call(functools.partial(kernel, toks, lanes, window), out_shape=...]
where the time goes in v1:
time: 85.1 us; the launch traced here: 85 us
  Pallas kernels  84.4 us (99%)
    pallas_call x1, Pallas kernels, shards(): pl.pallas_call(functools.partial(kernel, toks, lanes, window), out_shape=...  81.9 us
    pallas_call x1, Pallas kernels, shards(): pl.pallas_call(hand_over, out_shape=tuple((jax.ShapeDtypeStruct(r.shape,...  2.41 us

profile of v1, /device:TPU:0, one launch (start us, length us, event | category | flops | bytes accessed | tf_op | source)
XLA Modules:
  0.0 85.0 jit_solution(3717246158668860059)
XLA Ops:
  0.6 81.9 %shard_map.103 = (bf16[128,1024]{1,0:T(8,128)(2,1)}, bf16[128,4096]{1,0:T(8,128)(2,1)}, f32[128,512]{1,0:T(8,128)}) custom-call(bf16[128,4096]{1,0:T(8,128)(2,1)} %x_hbm.1, f32[128,508]{1,0:T(8,128)} %gate_hbm.1, bf16[128,1024]{1,0:T(8,128)(2,1)} %latin_hbm.1, bf16[128,1024]{1,0:T(8,128)(2,1)} %latgrad_hbm.1, s32[22,1024]{1,0:T(8,128)} %bitcast.3, ...), custom_call_target="tpu_custom_call" | custom-call | tf_op jit(solution)/shard_map/pallas_call | solution.py:512
  82.6 2.4 %shard_map.104 = (bf16[128,1024]{1,0:T(8,128)(2,1)}, bf16[128,4096]{1,0:T(8,128)(2,1)}, f32[128,512]{1,0:T(8,128)}) custom-call(bf16[128,1024]{1,0:T(8,128)(2,1)} %get-tuple-element.6.refs_0_, bf16[128,4096]{1,0:T(8,128)(2,1)} %get-tuple-element.7.refs_1_, f32[128,512]{1,0:T(8,128)} %get-tuple-element.8.refs_2_), custom_call_target="tpu_custom_call" | custom-call | tf_op jit(solution)/shard_map/pallas_call | solution.py:581

commit v2 on v1

--- a/solution.py
+++ b/solution.py
@@ -18,11 +18,11 @@
     x_hbm, gate_hbm, latin_hbm, latgrad_hbm, picks_hbm, rw_hbm, win_hbm, wout_hbm,
     latent_hbm, xgrad_hbm, rwg_out,
     x_ref, gate_ref, picks_ref, latent_out, xgrad_out,
-    rw, win, wout, lat, probs, pick_recv, pick_send, gate_recv, gate_send, gate_rows, gate_grads, hits_ref, own_hits_ref, rank, packed, active_ref,
+    rw, win, wout, lat, held_all, pick_recv, pick_send, gate_recv, gate_send, gate_rows, rows_recv, gate_grads, hits_ref, own_hits_ref, rank, packed, active_ref,
     term_send, term_recv, xband, xturned, logits_all, part, ax_send, ax_recv,
     bz_send, bz_recv, bx_send, bx_recv, az_send, az_recv, total_a, total_b,
     load_sem, send_lat, chain_ss, recv_z, recv_x, pick_ss, pick_rs, gate_ss, gate_rs, term_ss, term_rs,
-    band_ss, band_rs, log_ss, log_rs, ax_ss, ax_rs, bz_ss, bz_rs, bx_ss, bx_rs,
+    band_ss, band_rs, log_ss, log_rs, held_ss, held_rs, ax_ss, ax_rs, bz_ss, bz_rs, bx_ss, bx_rs,
     az_ss, az_rs,
 ):
     tok = lax.axis_index("tok")
@@ -140,14 +140,32 @@
     rest = gate_ref.shape[1]
     gate_grads[:, rest - rest % 128:] = jnp.zeros_like(gate_grads[:, rest - rest % 128:])
     gate_grads[:, :rest] = gate_ref[...]
-    gate_grads[...] = pltpu.roll(gate_grads[...], window, 1)
+    held_all[1, tok] = pltpu.roll(gate_grads[...], window, 1)
+    sibling = tok + 1 - 2 * lax.rem(tok, 2)
+
+    def held_copy(which, to_sibling, k):
+        far = lax.rem(tok + 2 * k, toks)
+        src = far if to_sibling else tok
+        sem = (toks // 2 + k) if to_sibling else (toks // 2 - k) % (toks // 2)
+        return pltpu.make_async_remote_copy(
+            src_ref=held_all.at[which, src], dst_ref=held_all.at[which, src],
+            send_sem=held_ss.at[which, toks // 2 + k if to_sibling else k], recv_sem=held_rs.at[which, sem],
+            device_id={"tok": sibling if to_sibling else far}, device_id_type=MESH,
+        )
+
+    def held_start(which):
+        for k in range(1, toks // 2):
+            held_copy(which, False, k).start()
+        held_copy(which, True, 0).start()
+
+    held_start(1)
 
     loads[0].wait()
     logits = jnp.dot(x_ref[...], rw[...], preferred_element_type=F32)
     shifted = jnp.exp(logits - jnp.max(logits, axis=1, keepdims=True))
-    probs[...] = shifted / jnp.sum(shifted, axis=1, keepdims=True)
+    held_all[0, tok] = shifted / jnp.sum(shifted, axis=1, keepdims=True)
     pad = own_hits_ref.shape[0]
-    pick_send[...] = jnp.transpose(probs[:, :128])[:pad] * own_hits_ref[...]
+    pick_send[...] = jnp.transpose(held_all[0, tok, :, :128])[:pad] * own_hits_ref[...]
     pick_recv[0] = pick_send[...]
 
     def pick_copy(k):
@@ -159,6 +177,7 @@
 
     for k in range(1, lanes):
         pick_copy(k).start()
+    held_start(0)
     before = (
         lax.broadcasted_iota(jnp.int32, (rows, rows), 0)
         <= lax.broadcasted_iota(jnp.int32, (rows, rows), 1)
@@ -256,6 +275,10 @@
 
         @pl.when(step == outers - 1)
         def _():
+            for which in range(2):
+                for k in range(toks // 2 - 1, 0, -1):
+                    held_copy(which, False, toks // 2 - k).wait_recv()
+                    held_copy(which, True, k).start()
             for k in range(toks):
                 if k:
                     band_copy(k).wait_recv()
@@ -275,28 +298,26 @@
         ).wait_recv()
     gate_rows[...] = jnp.zeros_like(gate_rows)
     for e in range(window):
-        gate_rows[e:e + 1, :] = gate_recv[2 * e, 0:1, :] + gate_recv[2 * e + 1, 0:1, :]
-    gate_grads[:, :128] = gate_grads[:, :128] + jnp.transpose(gate_rows[...])
-    gate_grad = gate_grads[...]
-    prob = probs[...]
-    centre = jnp.sum(prob * gate_grad, axis=1, keepdims=True)
-    logit_low = (prob * (gate_grad - centre)).astype(BF16)
-    logits_all[tok] = logit_low
-    sibling = tok + 1 - 2 * lax.rem(tok, 2)
-
-    def logit_copy(to_sibling, k):
-        far = lax.rem(tok + 2 * k, toks)
-        src = far if to_sibling else tok
-        sem = (toks // 2 + k) if to_sibling else (toks // 2 - k) % (toks // 2)
-        return pltpu.make_async_remote_copy(
-            src_ref=logits_all.at[src], dst_ref=logits_all.at[src],
-            send_sem=log_ss.at[toks // 2 + k if to_sibling else k], recv_sem=log_rs.at[sem],
-            device_id={"tok": sibling if to_sibling else far}, device_id_type=MESH,
-        )
-
-    for k in range(1, toks // 2):
-        logit_copy(False, k).start()
-    logit_copy(True, 0).start()
+        gate_rows[tok, e:e + 1, :] = gate_recv[2 * e, 0:1, :] + gate_recv[2 * e + 1, 0:1, :]
+
+    def row_copy(k):
+        return pltpu.make_async_remote_copy(
+            src_ref=gate_rows.at[tok, pl.ds(0, pad)], dst_ref=rows_recv.at[tok],
+            send_sem=log_ss.at[k], recv_sem=log_rs.at[toks - k],
+            device_id={"tok": at_tok(k)}, device_id_type=MESH,
+        )
+
+    for k in range(1, toks):
+        row_copy(k).start()
+
+    def logit_rows(t):
+        head = held_all[1, t, :, :128] + jnp.transpose(gate_rows[t])
+        gate_grad = jnp.concatenate([head, held_all[1, t, :, 128:]], axis=1)
+        prob = held_all[0, t]
+        centre = jnp.sum(prob * gate_grad, axis=1, keepdims=True)
+        logits_all[t] = (prob * (gate_grad - centre)).astype(BF16)
+
+    logit_rows(tok)
 
     terms = jnp.dot(
         packed[...].reshape(lanes * SLOTS, packed.shape[2]), win[...], preferred_element_type=F32
@@ -314,11 +335,18 @@
         term_copy(k).start()
     term_recv[lane] = term_send[lane]
 
-    for k in range(toks // 2 - 1, 0, -1):
-        logit_copy(False, toks // 2 - k).wait_recv()
-        logit_copy(True, k).start()
-    for k in range(toks // 2):
-        logit_copy(True, k).wait_recv()
+    for which in range(2):
+        for k in range(toks // 2):
+            held_copy(which, True, k).wait_recv()
+    for k in range(1, toks):
+        peer = at_tok(k)
+        pltpu.make_async_remote_copy(
+            src_ref=gate_rows.at[tok, pl.ds(0, pad)], dst_ref=rows_recv.at[peer],
+            send_sem=log_ss.at[k], recv_sem=log_rs.at[k],
+            device_id={"tok": peer}, device_id_type=MESH,
+        ).wait_recv()
+        gate_rows[peer, :pad] = rows_recv[peer]
+        logit_rows(peer)
 
     experts = rw.shape[1]
     part[...] = jnp.dot(
@@ -440,7 +468,7 @@
     ).astype(BF16)
 
     stores[0].start()
-    xgrad_out[...] = lax.dot_general(logit_low, rw[...], NT, preferred_element_type=F32).astype(BF16)
+    xgrad_out[...] = lax.dot_general(logits_all[tok], rw[...], NT, preferred_element_type=F32).astype(BF16)
     stores[1].start()
 
     ax_wait(outer)
@@ -470,10 +498,13 @@
     line_sent(*line_b)
     line_sent(*line_a)
     bx.wait_send()
-    for k in range(toks // 2):
-        logit_copy(True, k).wait_send()
-        if k:
-            logit_copy(False, k).wait_send()
+    for k in range(1, toks):
+        row_copy(k).wait_send()
+    for which in range(2):
+        for k in range(toks // 2):
+            held_copy(which, True, k).wait_send()
+            if k:
+                held_copy(which, False, k).wait_send()
 
 
 def hand_over(*refs):
@@ -528,12 +559,13 @@
             pltpu.VMEM((hidden, latent), BF16),
             pltpu.VMEM((hidden, latent), BF16),
             pltpu.VMEM((2, lanes, rows, latent), BF16),
-            pltpu.VMEM((rows, experts), F32),
+            pltpu.VMEM((2, toks, rows, experts), F32),
             pltpu.VMEM((lanes, pad, rows), F32),
             pltpu.VMEM((pad, rows), F32),
             pltpu.VMEM((lanes, 8, rows), F32),
             pltpu.VMEM((lanes, 8, rows), F32),
-            pltpu.VMEM((128, rows), F32),
+            pltpu.VMEM((toks, 128, rows), F32),
+            pltpu.VMEM((toks, pad, rows), F32),
             pltpu.VMEM((rows, experts), F32),
             pltpu.VMEM((lanes, rows), F32),
             pltpu.VMEM((pad, rows), F32),
@@ -566,6 +598,7 @@
             dma((lanes,)), dma((lanes,)),
             dma((toks,)), dma((toks,)),
             dma((toks,)), dma((toks,)),
+            dma((2, toks)), dma((2, toks)),
             dma((outers,)), dma((outers,)),
             dma((2, outers)), dma((2, outers)),
             dma, dma,

time: 85.1 us -> 82.7 us (0.972)
  Pallas kernels: 84.4 us -> 81.9 us
    pallas_call x1, Pallas kernels: 81.9 us -> 79.5 us  [shards(): pl.pallas_call(functools.partial(kernel, toks, lanes, window), out_shape=...]
where the time goes in v2:
time: 82.7 us; the launch traced here: 82.6 us
  Pallas kernels  81.9 us (99%)
    pallas_call x1, Pallas kernels, shards(): pl.pallas_call(functools.partial(kernel, toks, lanes, window), out_shape=...  79.5 us
    pallas_call x1, Pallas kernels, shards(): pl.pallas_call(hand_over, out_shape=tuple((jax.ShapeDtypeStruct(r.shape,...  2.41 us

profile of v2, /device:TPU:0, one launch (start us, length us, event | category | flops | bytes accessed | tf_op | source)
XLA Modules:
  0.0 82.6 jit_solution(360220409617604528)
XLA Ops:
  0.6 79.5 %shard_map.103 = (bf16[128,1024]{1,0:T(8,128)(2,1)}, bf16[128,4096]{1,0:T(8,128)(2,1)}, f32[128,512]{1,0:T(8,128)}) custom-call(bf16[128,4096]{1,0:T(8,128)(2,1)} %x_hbm.1, f32[128,508]{1,0:T(8,128)} %gate_hbm.1, bf16[128,1024]{1,0:T(8,128)(2,1)} %latin_hbm.1, bf16[128,1024]{1,0:T(8,128)(2,1)} %latgrad_hbm.1, s32[22,1024]{1,0:T(8,128)} %bitcast.3, ...), custom_call_target="tpu_custom_call" | custom-call | tf_op jit(solution)/shard_map/pallas_call | solution.py:543
  80.2 2.4 %shard_map.104 = (bf16[128,1024]{1,0:T(8,128)(2,1)}, bf16[128,4096]{1,0:T(8,128)(2,1)}, f32[128,512]{1,0:T(8,128)}) custom-call(bf16[128,1024]{1,0:T(8,128)(2,1)} %get-tuple-element.6.refs_0_, bf16[128,4096]{1,0:T(8,128)(2,1)} %get-tuple-element.7.refs_1_, f32[128,512]{1,0:T(8,128)} %get-tuple-element.8.refs_2_), custom_call_target="tpu_custom_call" | custom-call | tf_op jit(solution)/shard_map/pallas_call | solution.py:614

commit v3 on v2

--- a/solution.py
+++ b/solution.py
@@ -534,7 +534,7 @@
     feats = width // toks
     own_rows = feats // lanes
     outers = lanes // 2
-    half = max(16, own_rows * 3 // 4 // 16 * 16)
+    half = max(16, own_rows * 7 // 8 // 16 * 16)
     tail = own_rows - half
     pad = -(-window // 8) * 8
     vmem = pl.BlockSpec(memory_space=pltpu.VMEM)

time: 82.7 us -> 82.4 us (level)
  no operation moved by 1% of the time
where the time goes in v3:
time: 82.4 us; the launch traced here: 82.3 us
  Pallas kernels  81.6 us (99%)
    pallas_call x1, Pallas kernels, shards(): pl.pallas_call(functools.partial(kernel, toks, lanes, window), out_shape=...  79.2 us
    pallas_call x1, Pallas kernels, shards(): pl.pallas_call(hand_over, out_shape=tuple((jax.ShapeDtypeStruct(r.shape,...  2.41 us

profile of v3, /device:TPU:0, one launch (start us, length us, event | category | flops | bytes accessed | tf_op | source)
XLA Modules:
  0.0 82.3 jit_solution(640292883076019598)
XLA Ops:
  0.6 79.2 %shard_map.103 = (bf16[128,1024]{1,0:T(8,128)(2,1)}, bf16[128,4096]{1,0:T(8,128)(2,1)}, f32[128,512]{1,0:T(8,128)}) custom-call(bf16[128,4096]{1,0:T(8,128)(2,1)} %x_hbm.1, f32[128,508]{1,0:T(8,128)} %gate_hbm.1, bf16[128,1024]{1,0:T(8,128)(2,1)} %latin_hbm.1, bf16[128,1024]{1,0:T(8,128)(2,1)} %latgrad_hbm.1, s32[22,1024]{1,0:T(8,128)} %bitcast.3, ...), custom_call_target="tpu_custom_call" | custom-call | tf_op jit(solution)/shard_map/pallas_call | solution.py:543
  79.8 2.4 %shard_map.104 = (bf16[128,1024]{1,0:T(8,128)(2,1)}, bf16[128,4096]{1,0:T(8,128)(2,1)}, f32[128,512]{1,0:T(8,128)}) custom-call(bf16[128,1024]{1,0:T(8,128)(2,1)} %get-tuple-element.6.refs_0_, bf16[128,4096]{1,0:T(8,128)(2,1)} %get-tuple-element.7.refs_1_, f32[128,512]{1,0:T(8,128)} %get-tuple-element.8.refs_2_), custom_call_target="tpu_custom_call" | custom-call | tf_op jit(solution)/shard_map/pallas_call | solution.py:614
